TPU v7x, 32 devices: a whole 2x2x4 slice. The times are simulated.
32 devices in a mesh: groups: 2 (over x), wide: 8 (over z, y), hid: 2 (over core).
Axes of the slice: x: 2, y: 2, z: 4, core: 2. Of those that a mesh axis runs over, the one named last changes fastest.
Arguments:
- tokens: bfloat16 [4096, 7168], P(('groups', 'hid'), 'wide'), parts along dimension 0, may hold values from -6 to 6
- expert_ids: int32 [4096, 2], P('groups'), parts along dimension 0, may hold values from 0 to 15, all different within a row; in each aligned block of 2048 rows (0 to 2047, 2048 to 4095, ...) at most 384 rows name the same one
- gate_scale: float32 [4096, 2], P('groups'), parts along dimension 0, may hold values from 0.2 to 1
- gate_weight: bfloat16 [16, 7168, 1024], P(None, 'wide', 'hid'), may hold values from -0.0625 to 0.0625
- up_weight: bfloat16 [16, 7168, 1024], P(None, 'wide', 'hid'), may hold values from -0.0625 to 0.0625
- down_weight: bfloat16 [16, 1024, 7168], P(None, 'hid', 'wide'), may hold values from -0.1875 to 0.1875
Outputs:
- layer_output: bfloat16 [4096, 7168], P(('groups', 'hid'), 'wide'), parts along dimension 0
There are 2 independent parts, one for each index of `groups`. A program takes and returns all parts, laid end to end along the dimension named above; an argument that names none is the same for every part. Nothing has to cross between parts.
Inputs may be any that keep to these rules, and one draw needn't show every extreme that they name: `expert_ids`: the 2 entries of a token are different experts. In each part no expert is named by more than 384 tokens, a bound that some block reaches; every expert is named by some token.
All inputs are finite; a program needn't handle non-finite values.
Results may differ from a plain program's by a relative error of at most 0.02.
Values may be sent and summed in bfloat16 or wider, within the bound.
A program may use at most 192 MiB of HBM per device.

v0:
```python
import jax
import jax.numpy as jnp
from jax import lax
from jax.sharding import PartitionSpec as P

block_rows = 128


def pick_group(blocks):
    for size_try in (8, 4, 2):
        if blocks % size_try == 0:
            return size_try
    return 1


def grouped_product(row_data, labels, first_weight, second_weight):
    blocks = row_data.shape[0] // block_rows
    per_step = pick_group(blocks)
    shaped = row_data.reshape(blocks // per_step, per_step, block_rows, row_data.shape[1])
    label_groups = labels.reshape(blocks // per_step, per_step)

    def advance(state_in, operands):
        row_group, label_group = operands
        results = []
        for j in range(per_step):
            weight_one = lax.dynamic_index_in_dim(first_weight, label_group[j], 0, keepdims=False)
            product = jnp.dot(row_group[j], weight_one, preferred_element_type=jnp.float32)
            if second_weight is not None:
                weight_two = lax.dynamic_index_in_dim(
                    second_weight, label_group[j], 0, keepdims=False
                )
                second_part = jnp.dot(row_group[j], weight_two, preferred_element_type=jnp.float32)
                product = jnp.concatenate([product, second_part], axis=1)
            results.append(product)
        return (state_in, jnp.stack(results))

    _, stacked = lax.scan(advance, jnp.int32(0), (shaped, label_groups))
    return stacked.reshape(row_data.shape[0], stacked.shape[-1])


def routing_tables(expert_ids, experts, capacity, block_total):
    flat_ids = expert_ids.reshape(-1)
    labels = jnp.arange(experts, dtype=jnp.int32)
    onehot = (flat_ids[:, None] == labels[None, :]).astype(jnp.int32)
    slot_rank = jnp.sum((jnp.cumsum(onehot, axis=0) - onehot) * onehot, axis=1)
    block_index = jnp.arange(block_total, dtype=jnp.int32)
    row_start = labels * capacity
    block_expert = block_index * block_rows // capacity
    row_index = jnp.sum(onehot * row_start[None, :], axis=1) + slot_rank
    owner_token = jnp.arange(flat_ids.shape[0], dtype=jnp.int32) // expert_ids.shape[1]
    source = jnp.zeros((block_total * block_rows,), jnp.int32).at[row_index].set(owner_token)
    return (row_index.reshape(expert_ids.shape), source, block_expert)


def body(tokens, expert_ids, gate_scale, gate_weight, up_weight, down_weight):
    token_total, slot_count = expert_ids.shape
    experts = gate_weight.shape[0]
    half_hidden = gate_weight.shape[2]
    capacity = (
        (token_total * slot_count * 3 // (2 * experts) + block_rows - 1) // block_rows * block_rows
    )
    block_total = experts * capacity // block_rows
    row_index, source, block_expert = routing_tables(expert_ids, experts, capacity, block_total)
    features = lax.all_gather(tokens, "hid", axis=0, tiled=True)
    labels = block_expert
    summed = lax.psum_scatter(
        grouped_product(jnp.take(features, source, axis=0), labels, gate_weight, up_weight).astype(
            jnp.bfloat16
        ),
        "wide",
        scatter_dimension=0,
        tiled=True,
    ).astype(jnp.float32)
    hidden = (jax.nn.silu(summed[:, :half_hidden]) * summed[:, half_hidden:]).astype(jnp.bfloat16)
    row_expert = jnp.repeat(block_expert, block_rows)

    def project_down(hidden_rows, offset):
        length = hidden_rows.shape[0]
        if length % block_rows == 0:
            labels = lax.dynamic_slice_in_dim(
                block_expert, offset // block_rows, length // block_rows
            )
            return grouped_product(hidden_rows, labels, down_weight, None)
        row_labels = lax.dynamic_slice_in_dim(row_expert, offset, length)

        def add_expert(expert_index, running):
            weight_one = lax.dynamic_index_in_dim(down_weight, expert_index, 0, keepdims=False)
            chosen = (row_labels == expert_index)[:, None]
            product = jnp.dot(hidden_rows, weight_one, preferred_element_type=jnp.float32)
            return running + jnp.where(chosen, product, 0.0)

        return lax.fori_loop(
            0, experts, add_expert, jnp.zeros((length, down_weight.shape[2]), jnp.float32)
        )

    down_rows = project_down(lax.all_gather(hidden, "wide", axis=0, tiled=True), jnp.int32(0))
    picked = jnp.take(down_rows, row_index, axis=0)
    combined = jnp.sum(gate_scale[:, :, None] * picked, axis=1)
    return lax.psum_scatter(combined.astype(jnp.bfloat16), "hid", scatter_dimension=0, tiled=True)


def solution(mesh):
    placed = (
        P(("groups", "hid"), "wide"),
        P("groups", None),
        P("groups", None),
        P(None, "wide", "hid"),
        P(None, "wide", "hid"),
        P(None, "hid", "wide"),
    )
    return jax.shard_map(
        body, mesh=mesh, in_specs=placed, out_specs=P(("groups", "hid"), "wide"), check_vma=False
    )
```

profile of v0, /device:TPU:0, one launch (start us, length us, event | category | flops | bytes accessed | tf_op | source)
XLA Modules:
  0.0 976.3 jit_solution(15945626137611912277)
XLA Ops:
  9.4 4.6 reduce-window.6
  15.1 15.5 %scatter_custom_fusion = s32[6144]{0:T(1024)S(1)} fusion(s32[4096]{0:T(1024)S(1)} %bitcast.411, s32[4096]{0:T(1024)S(1)} %add_select_fusion, s32[]{:T(128)} %constant.148.clone.1), kind=kCustom, calls=%fused_computation.171 | custom fusion | bytes 24580 | tf_op jit(solution)/shard_map/scatter | solution.py:51
  30.7 31.8 %gather_fusion = bf16[6144,896]{1,0:T(8,128)(2,1)} fusion(bf16[2048,896]{1,0:T(8,128)(2,1)} %all-gather.3.cloned.1.call-done, s32[6144]{0:T(1024)S(1)} %fusion.109), kind=kCustom, calls=%fused_computation | custom fusion | bytes 22044672 | tf_op jit(solution)/shard_map/jit(_take)/gather | solution.py:67
  62.5 10.0 %broadcast_select_fusion = bf16[6,8,128,896]{3,2,1,0:T(8,128)(2,1)} fusion(bf16[6,8,128,896]{3,2,1,0:T(8,128)(2,1)} %bitcast.405, pred[6,8,128]{2,1,0:T(8,128)(4,1)S(1)} %and_bitcast_fusion), kind=kLoop, calls=%fused_computation.144 | loop fusion | flops 5505024 | bytes 22026240 | tf_op jit(solution)/shard_map/jit(_take)/select_n | solution.py:67
  72.5 261.5 %while.20 = (s32[]{:T(128)}, bf16[6,8,128,1024]{3,2,1,0:T(8,128)(2,1)}, bf16[6,8,128,896]{3,2,1,0:T(8,128)(2,1)}, s32[6,8]{1,0:T(8,128)S(1)}, bf16[16,896,512]{2...) while((s32[]{:T(128)}, ...), condition=%wide.region_6.7_spmd, body=%wide.region_5.6_spmd.sunk | while | flops 1883242496 | bytes 28845296 | solution.py:37
  334.1 210.1 %reduce-scatter.3.cloned.1.call-done = bf16[768,1024]{1,0:T(8,128)(2,1)} async-done(((bf16[6144,1024]{1,0:T(8,128)(2,1)}), bf16[768,1024]{1,0:T(8,128)(2,1)}) %reduce-scatter.3.cloned.1.call-update) | async-done | bytes 1572880 | tf_op jit(solution)/shard_map/reduce_scatter | solution.py:66
  551.0 94.7 %all-gather.5.cloned.1.call-done = bf16[6144,512]{1,0:T(8,128)(2,1)} async-done(((bf16[768,512]{1,0:T(8,128)(2,1)}), bf16[6144,512]{1,0:T(8,128)(2,1)}) %all-gather.5.cloned.1.call-update) | async-done | bytes 6291472 | tf_op jit(solution)/shard_map/all_gather | solution.py:96
  645.7 235.0 %while.21 = (s32[]{:T(128)}, f32[6,8,128,896]{3,2,1,0:T(8,128)}, bf16[6,8,128,512]{3,2,1,0:T(8,128)(2,1)}, s32[6,8]{1,0:T(8,128)S(1)}, bf16[16,512,896]{2,1,0:T(...) while((s32[]{:T(128)}, f32[6,8,128,896]{3,2,1,0:T(8,128)}, ...), condition=%wide.region_9.10_spmd, body=%wide.region_8.9_spmd.sunk | while | flops 939524096 | bytes 19403952 | solution.py:37
  648.4 2.4 fusion.226
  657.0 2.4 fusion.228
  661.2 2.4 fusion.229
  665.3 2.4 fusion.230
  669.6 2.4 fusion.231
  678.3 2.4 fusion.233
  680.7 4.1 bitcast_dynamic-update-slice_fusion.5
  687.5 2.4 fusion.226
  696.1 2.4 fusion.228
  700.4 2.4 fusion.229
  704.4 2.4 fusion.230
  717.4 2.4 fusion.233
  719.8 4.2 bitcast_dynamic-update-slice_fusion.5
  726.7 2.4 fusion.226
  735.2 2.4 fusion.228
  739.5 2.4 fusion.229
  743.6 2.4 fusion.230
  756.6 2.4 fusion.233
  759.0 4.2 bitcast_dynamic-update-slice_fusion.5
  765.9 2.4 fusion.226
  774.5 2.4 fusion.228
  778.7 2.4 fusion.229
  782.8 2.4 fusion.230
  795.8 2.4 fusion.233
  798.2 4.2 bitcast_dynamic-update-slice_fusion.5
  813.7 2.4 fusion.228
  818.0 2.4 fusion.229
  822.1 2.4 fusion.230
  835.0 2.4 fusion.233
  837.4 4.1 bitcast_dynamic-update-slice_fusion.5
  844.2 2.4 fusion.226
  852.8 2.4 fusion.228
  857.1 2.4 fusion.229
  861.2 2.4 fusion.230
  874.1 2.4 fusion.233
  876.5 4.2 bitcast_dynamic-update-slice_fusion.5
  880.7 28.4 %gather_fusion.1 = f32[4096,896]{1,0:T(8,128)} fusion(f32[6144,896]{1,0:T(8,128)} %bitcast.404, s32[4096]{0:T(1024)S(1)} %broadcast_clamp_fusion), kind=kCustom, calls=%fused_computation.1 | custom fusion | bytes 29376512 | tf_op jit(solution)/shard_map/jit(_take)/gather | solution.py:97
  909.1 17.4 %reshape.182 = f32[2048,2,896]{2,1,0:T(2,128)} reshape(f32[4096,896]{1,0:T(8,128)} %gather_fusion.1) | data formatting | bytes 29360128 | tf_op jit(solution)/shard_map/jit(_take)/gather | solution.py:97
  926.5 33.4 %multiply_reduce_fusion = bf16[2048,896]{1,0:T(8,128)(2,1)} fusion(f32[2048,2,896]{2,1,0:T(2,128)} %reshape.182, pred[2048,2]{1,0:T(8,128)(4,1)S(1)} %compare_and_fusion, f32[2048,2]{1,0:T(8,128)S(1)} %copy.8), kind=kLoop, calls=%fused_computation.143 | loop fusion | flops 9175040 | bytes 18370560 | tf_op jit(solution)/shard_map/reduce_sum | solution.py:98
  959.8 9.9 %reduce-scatter.5.cloned.1.call-done = bf16[1024,896]{1,0:T(8,128)(2,1)} async-done(((bf16[2048,896]{1,0:T(8,128)(2,1)}), bf16[1024,896]{1,0:T(8,128)(2,1)}) %reduce-scatter.5.cloned.1.call-update) | async-done | bytes 1835024 | tf_op jit(solution)/shard_map/reduce_scatter | solution.py:99
  (229 shorter events, 227.1 us)
Async XLA Ops:
  6.5 24.2 %all-gather.3.cloned.1.call-start = ((), (), s32[]{:S(2)}) async-start(), calls=%async_computation.2 | async-start | bytes 5505024 | tf_op jit(solution)/shard_map/all_gather | solution.py:64
  7.3 536.9 %reduce-scatter.3.cloned.1.call-start = ((), (), s32[]{:S(2)}) async-start(), calls=%async_computation.3 | async-start | bytes 14155776 | tf_op jit(solution)/shard_map/reduce_scatter | solution.py:66
  334.0 216.3 %copy-start = (f32[2048,2]{0,1:T(2,128)S(1)}, f32[2048,2]{0,1:T(2,128)}, u32[]{:S(2)}) copy-start(f32[2048,2]{0,1:T(2,128)} %param.12) | copy-start | bytes 49156
  334.0 311.7 %all-gather.5.cloned.1.call-start = ((), (), s32[]{:S(2)}) async-start(), calls=%async_computation.4 | async-start | bytes 7077888 | tf_op jit(solution)/shard_map/all_gather | solution.py:96
  547.4 422.3 %reduce-scatter.5.cloned.1.call-start = ((), (), s32[]{:S(2)}) async-start(), calls=%async_computation.5 | async-start | bytes 5505024 | tf_op jit(solution)/shard_map/reduce_scatter | solution.py:99
Sparse Core Ops, SparseCore 0:
  8.9 15.5 all-gather.2
  334.1 210.0 reduce-scatter.2
  547.5 98.1 all-gather.4
  960.0 9.7 reduce-scatter.4
where the time goes:
time: 983 us; the launch traced here: 976 us
  waiting for transfers between devices  316 us (32%)
  matrix products  269 us (27%)
  loops' own time  184 us (19%)
  local copies, waits for them, and re-layouts  141 us (14%)
  other arithmetic  53.2 us (5%)
  between operations  13.3 us (1%)
    reduce_scatter x1, waiting for transfers between devices, body(): lax.psum_scatter(grouped_product(jnp.take(features, source, axis=0), labe...  210 us
    dot_general x96, matrix products, advance(): jnp.dot(row_group[j], weight_one, preferred_element_type=jnp.float32)  191 us
    another operation x2, loops' own time, grouped_product(): _, stacked = lax.scan(advance, jnp.int32(0), (shaped, label_groups))  184 us
    all_gather x1, waiting for transfers between devices, body(): lax.all_gather(hidden, 'wide', axis=0, tiled=True)  94.7 us
    dot_general x48, matrix products, advance(): jnp.dot(row_group[j], weight_two, preferred_element_type=jnp.float32)  77.7 us
    gather x2, local copies, waits for them, and re-layouts, body(): picked = jnp.take(down_rows, row_index, axis=0)  45.8 us
    dynamic_update_slice x12, local copies, waits for them, and re-layouts, grouped_product(): _, stacked = lax.scan(advance, jnp.int32(0), (shaped, label_groups))  34.8 us
    reduce_sum x1, other arithmetic, body(): combined = jnp.sum(gate_scale[:, :, None] * picked, axis=1)  33.4 us
  transfers between devices with their start and end apart: 4, of which 3 were waited for; matrix products, arithmetic and copies ran while one was open for 3% of the time, Pallas kernels for 0%

commit v1 on v0

v1 whole, which is shorter than its diff:
```python
import functools

import jax
import jax.numpy as jnp
from jax import lax
from jax.experimental import pallas as pl
from jax.experimental.pallas import tpu as pltpu
from jax.sharding import PartitionSpec as P

row_align = 16
lane_width = 128
gather_rows = 256
vmem_bytes = 60 * 1024 * 1024


def round_up(value, unit):
    return (value + unit - 1) // unit * unit


def routing_tables(expert_ids, experts):
    flat_ids = expert_ids.reshape(-1)
    labels = jnp.arange(experts, dtype=jnp.int32)
    onehot = (labels[:, None] == flat_ids[None, :]).astype(jnp.int32)
    running = jnp.cumsum(onehot, axis=1)
    counts = running[:, -1]
    padded = (counts + row_align - 1) // row_align * row_align
    starts = jnp.sum(jnp.where(labels[None, :] < labels[:, None], padded[None, :], 0), axis=1)
    place = jnp.sum(onehot * (running - 1 + starts[:, None]), axis=0)
    return place.reshape(expert_ids.shape), jnp.concatenate([starts, counts]).astype(jnp.int32)


def up_kernel(experts, real_rows, rows, block, table, place, tokens, gate, up, out, gathered):
    expert = pl.program_id(0)

    @pl.when(expert == 0)
    def _():
        tail = gathered.shape[0] - rows
        gathered[rows:, :] = jnp.zeros((tail, gathered.shape[1]), gathered.dtype)
        rest = out.shape[1] - real_rows
        out[:, real_rows:, :] = jnp.zeros((out.shape[0], rest, out.shape[2]), out.dtype)
        first, second = place[0:1, :], place[1:2, :]

        def gather(step, carry):
            base = pl.multiple_of(step * gather_rows, gather_rows)
            ids = lax.broadcasted_iota(jnp.int32, (gather_rows, tokens.shape[0]), 0) + base
            chosen = jnp.where((ids == first) | (ids == second), 1.0, 0.0).astype(jnp.bfloat16)
            picked = jnp.dot(chosen, tokens[...], preferred_element_type=jnp.float32)
            gathered[pl.ds(base, gather_rows), :] = picked.astype(jnp.bfloat16)
            return carry

        lax.fori_loop(0, rows // gather_rows, gather, 0)

    start, count = table[expert], table[experts + expert]

    def multiply(step, carry):
        base = pl.multiple_of(start + step * block, row_align)
        part = gathered[pl.ds(base, block), :]
        gates = jnp.dot(part, gate[0], preferred_element_type=jnp.float32).astype(jnp.bfloat16)
        ups = jnp.dot(part, up[0], preferred_element_type=jnp.float32).astype(jnp.bfloat16)
        for s in range(out.shape[0]):
            cut = slice(s * lane_width, (s + 1) * lane_width)
            out[s, pl.ds(base, block), 0:lane_width] = gates[:, cut]
            out[s, pl.ds(base, block), lane_width:] = ups[:, cut]
        return carry

    lax.fori_loop(0, (count + block - 1) // block, multiply, 0)


def exchange_kernel(n, rows, partial, result, own, paired, summed, hidden, *sems):
    own_sem, y_send, y_recv, z_send, z_recv, g_send, g_recv, h_send, h_recv, out_sem = sems
    slices = own.shape[0]
    depth = n // 2
    chunk = rows // n
    half = rows // 2
    me = lax.axis_index("wide")
    y, z = lax.rem(me, 2), lax.div(me, 2)
    y_peer = {"wide": me + 1 - 2 * y}
    ahead = [{"wide": lax.rem(z + j, depth) * 2 + y} for j in range(depth)]
    mesh_type = pl.DeviceIdType.MESH

    own_base = pl.multiple_of(y * half, row_align)
    peer_base = pl.multiple_of((1 - y) * half, row_align)
    my_rows = pl.ds(pl.multiple_of(y * half + z * chunk, row_align), chunk)
    my_part = pl.ds(pl.multiple_of(z * chunk, row_align), chunk)

    def own_copy(s):
        return pltpu.make_async_copy(
            partial.at[s, pl.ds(own_base, half)], own.at[s], own_sem.at[s]
        )

    def y_copy(s):
        return pltpu.make_async_remote_copy(
            partial.at[s, pl.ds(peer_base, half)], paired.at[s],
            y_send.at[s], y_recv.at[s], y_peer, mesh_type,
        )

    def z_copy(s, j):
        part = pl.ds(pl.multiple_of(lax.rem(z + j, depth) * chunk, row_align), chunk)
        return pltpu.make_async_remote_copy(
            own.at[s, part], summed.at[s, j - 1],
            z_send.at[s, j - 1], z_recv.at[s, j - 1], ahead[j], mesh_type,
        )

    def g_copy(s, j):
        return pltpu.make_async_remote_copy(
            hidden.at[s, my_rows], hidden.at[s, my_rows],
            g_send.at[s, j - 1], g_recv.at[s, j - 1], ahead[j], mesh_type,
        )

    def h_copy(s):
        return pltpu.make_async_remote_copy(
            hidden.at[s, pl.ds(own_base, half)], hidden.at[s, pl.ds(own_base, half)],
            h_send.at[s], h_recv.at[s], y_peer, mesh_type,
        )

    def out_copy(s):
        return pltpu.make_async_copy(
            hidden.at[s], result.at[s, pl.ds(0, rows)], out_sem.at[s]
        )

    barrier = pltpu.get_barrier_semaphore()
    for peer in [y_peer] + ahead[1:]:
        pl.semaphore_signal(barrier, inc=1, device_id=peer, device_id_type=mesh_type)
    for s in range(slices):
        own_copy(s).start()
    pl.semaphore_wait(barrier, depth)
    for s in range(min(2, slices)):
        y_copy(s).start()
    far_first = sorted(range(1, depth), key=lambda j: -min(j, depth - j))

    for step in range(slices + 2):
        s = step
        if s < slices:
            own_copy(s).wait()
            y_copy(s).wait_recv()

            def add(j, carry, s=s):
                part = pl.ds(pl.multiple_of(j * chunk, row_align), chunk)
                own[s, part] = (
                    own[s, part].astype(jnp.float32) + paired[s, part].astype(jnp.float32)
                ).astype(jnp.bfloat16)
                return carry

            lax.fori_loop(0, depth, add, 0)
            for j in far_first:
                z_copy(s, j).start()
            if s + 2 < slices:
                y_copy(s + 2).start()
        s = step - 1
        if 0 <= s < slices:
            total = own[s, my_part].astype(jnp.float32)
            for j in far_first:
                z_copy(s, j).wait_recv()
            for j in range(1, depth):
                total = total + summed[s, j - 1].astype(jnp.float32)
            gates, ups = total[:, :lane_width], total[:, lane_width:]
            hidden[s, my_rows] = (gates / (1.0 + jnp.exp(-gates)) * ups).astype(jnp.bfloat16)
            for j in far_first:
                g_copy(s, j).start()
        s = step - 2
        if 0 <= s < slices:
            for j in far_first:
                g_copy(s, j).wait_recv()
            h_copy(s).start()
    for s in range(slices):
        h_copy(s).wait_recv()
        out_copy(s).start()
    for s in range(slices):
        y_copy(s).wait_send()
        for j in range(1, depth):
            z_copy(s, j).wait_send()
            g_copy(s, j).wait_send()
        h_copy(s).wait_send()
        out_copy(s).wait()


def down_kernel(experts, real_rows, rows, block, table, place, scale, hidden, weight, out, held):
    expert = pl.program_id(0)

    @pl.when(expert == 0)
    def _():
        rest = held.shape[0] - real_rows
        held[real_rows:, :] = jnp.zeros((rest, held.shape[1]), held.dtype)

    start, count = table[expert], table[experts + expert]

    def multiply(step, carry):
        base = pl.multiple_of(start + step * block, row_align)
        part = jnp.concatenate(
            [hidden[s, pl.ds(base, block), :] for s in range(hidden.shape[0])], axis=1
        )
        product = jnp.dot(part, weight[0], preferred_element_type=jnp.float32)
        held[pl.ds(base, block), :] = product.astype(jnp.bfloat16)
        return carry

    lax.fori_loop(0, (count + block - 1) // block, multiply, 0)

    @pl.when(expert == experts - 1)
    def _():
        def combine(step, carry):
            base = pl.multiple_of(step * gather_rows, gather_rows)
            span = pl.ds(base, gather_rows)
            ids = lax.broadcasted_iota(jnp.int32, (gather_rows, rows), 1)
            places, scales = place[span, :], scale[span, :]
            mixed = jnp.where(
                ids == places[:, 0:1], scales[:, 0:1],
                jnp.where(ids == places[:, 1:2], scales[:, 1:2], 0.0),
            ).astype(jnp.bfloat16)
            total = jnp.dot(mixed, held[0:rows, :], preferred_element_type=jnp.float32)
            out[span, :] = total.astype(jnp.bfloat16)
            return carry

        lax.fori_loop(0, out.shape[0] // gather_rows, combine, 0)


def whole_block(shape):
    return pl.BlockSpec(
        shape, lambda e, table: (0,) * len(shape), pipeline_mode=pl.Buffered(1)
    )


def body(n, tokens, expert_ids, gate_scale, gate_weight, up_weight, down_weight):
    token_total, slot_count = expert_ids.shape
    experts, width, half_hidden = gate_weight.shape
    slices = half_hidden // lane_width
    depth = n // 2
    real_rows = token_total * slot_count
    capacity = round_up(real_rows * 3 // (2 * experts), 2 * row_align)
    block = capacity // 2
    rows = round_up(real_rows + row_align * experts, max(n * row_align, gather_rows))
    chunk = rows // n
    all_rows = rows + capacity
    bf16 = jnp.bfloat16

    place, table = routing_tables(expert_ids, experts)
    features = lax.all_gather(tokens, "hid", axis=0, tiled=True)

    partial = pl.pallas_call(
        functools.partial(up_kernel, experts, real_rows, rows, block),
        out_shape=jax.ShapeDtypeStruct((slices, all_rows, 2 * lane_width), bf16),
        grid_spec=pltpu.PrefetchScalarGridSpec(
            num_scalar_prefetch=1,
            grid=(experts,),
            in_specs=[
                whole_block((slot_count, token_total)),
                whole_block((token_total, width)),
                pl.BlockSpec((1, width, half_hidden), lambda e, table: (e, 0, 0)),
                pl.BlockSpec((1, width, half_hidden), lambda e, table: (e, 0, 0)),
            ],
            out_specs=whole_block((slices, all_rows, 2 * lane_width)),
            scratch_shapes=[pltpu.VMEM((all_rows, width), bf16)],
        ),
        compiler_params=pltpu.CompilerParams(vmem_limit_bytes=vmem_bytes),
    )(table, place.T, features, gate_weight, up_weight)

    dma = pltpu.SemaphoreType.DMA
    hidden = pl.pallas_call(
        functools.partial(exchange_kernel, n, rows),
        out_shape=jax.ShapeDtypeStruct((slices, all_rows, lane_width), bf16),
        in_specs=[pl.BlockSpec(memory_space=pl.ANY)],
        out_specs=pl.BlockSpec(memory_space=pl.ANY),
        scratch_shapes=[
            pltpu.VMEM((slices, rows // 2, 2 * lane_width), bf16),
            pltpu.VMEM((slices, rows // 2, 2 * lane_width), bf16),
            pltpu.VMEM((slices, depth - 1, chunk, 2 * lane_width), bf16),
            pltpu.VMEM((slices, rows, lane_width), bf16),
            dma((slices,)),
            dma((slices,)),
            dma((slices,)),
            dma((slices, depth - 1)),
            dma((slices, depth - 1)),
            dma((slices, depth - 1)),
            dma((slices, depth - 1)),
            dma((slices,)),
            dma((slices,)),
            dma((slices,)),
        ],
        compiler_params=pltpu.CompilerParams(
            collective_id=0, has_side_effects=True, vmem_limit_bytes=vmem_bytes
        ),
    )(partial)

    combined = pl.pallas_call(
        functools.partial(down_kernel, experts, real_rows, rows, block),
        out_shape=jax.ShapeDtypeStruct((token_total, width), bf16),
        grid_spec=pltpu.PrefetchScalarGridSpec(
            num_scalar_prefetch=1,
            grid=(experts,),
            in_specs=[
                whole_block((token_total, slot_count)),
                whole_block((token_total, slot_count)),
                whole_block((slices, all_rows, lane_width)),
                pl.BlockSpec((1, half_hidden, width), lambda e, table: (e, 0, 0)),
            ],
            out_specs=whole_block((token_total, width)),
            scratch_shapes=[pltpu.VMEM((all_rows, width), bf16)],
        ),
        compiler_params=pltpu.CompilerParams(vmem_limit_bytes=vmem_bytes),
    )(table, place, gate_scale, hidden, down_weight)
    return lax.psum_scatter(combined, "hid", scatter_dimension=0, tiled=True)


def solution(mesh):
    placed = (
        P(("groups", "hid"), "wide"),
        P("groups", None),
        P("groups", None),
        P(None, "wide", "hid"),
        P(None, "wide", "hid"),
        P(None, "hid", "wide"),
    )
    return jax.shard_map(
        functools.partial(body, mesh.shape["wide"]),
        mesh=mesh,
        in_specs=placed,
        out_specs=P(("groups", "hid"), "wide"),
        check_vma=False,
    )
```

time: 983 us -> 329 us (0.33)
  waiting for transfers between devices: 316 us -> 21 us
  Pallas kernels: 0 us -> 281 us
  matrix products: 269 us -> 0 us
  loops' own time: 184 us -> 0 us
  local copies, waits for them, and re-layouts: 141 us -> 5.93 us
  other arithmetic: 53.2 us -> 5.86 us
    pallas_call x0 -> x3, Pallas kernels: none -> 281 us  [the longest x1 191 us: body(): pl.pallas_call(functools.partial(exchange_kernel, n, rows), out_shape=jax...]
    dot_general x144 -> x0, matrix products: 269 us -> none  [the longest x96 191 us: advance(): jnp.dot(row_group[j], weight_one, preferred_element_type=jnp.float32)]
    reduce_scatter x2 -> x1, waiting for transfers between devices: 220 us -> 14.9 us  [body(): return lax.psum_scatter(combined, 'hid', scatter_dimension=0, tiled=True)]
    another operation x2 -> x0, loops' own time: 184 us -> none  [grouped_product(): _, stacked = lax.scan(advance, jnp.int32(0), (shaped, label_groups))]
    all_gather x1 -> x0, waiting for transfers between devices: 94.7 us -> none  [body(): lax.all_gather(hidden, 'wide', axis=0, tiled=True)]
    gather x3 -> x0, local copies, waits for them, and re-layouts: 77.5 us -> none  [the longest x2 45.8 us: body(): picked = jnp.take(down_rows, row_index, axis=0)]
    dynamic_update_slice x12 -> x0, local copies, waits for them, and re-layouts: 34.8 us -> none  [grouped_product(): _, stacked = lax.scan(advance, jnp.int32(0), (shaped, label_groups))]
    reduce_sum x2, other arithmetic: 33.6 us -> 0.27 us  [the longest x1 0.16 us: routing_tables(): place = jnp.sum(onehot * (running - 1 + starts[:, None]), axis=0)]
  transfers between devices with their start and end apart: 4 -> 2, of which waited for: 3 -> 2; matrix products, arithmetic and copies ran while one was open for 3% -> 4% of each run, Pallas kernels for 0% -> 0%
where the time goes in v1:
time: 329 us; the launch traced here: 328 us
  Pallas kernels  281 us (85%)
  waiting for transfers between devices  21 us (6%)
  between operations  13.5 us (4%)
  local copies, waits for them, and re-layouts  5.93 us (2%)
  other arithmetic  5.86 us (2%)
    pallas_call x1, Pallas kernels, body(): pl.pallas_call(functools.partial(exchange_kernel, n, rows), out_shape=jax...  191 us
    pallas_call x1, Pallas kernels, body(): pl.pallas_call(functools.partial(up_kernel, experts, real_rows, rows, blo...  48.6 us
    pallas_call x1, Pallas kernels, body(): pl.pallas_call(functools.partial(down_kernel, experts, real_rows, rows, b...  41.3 us
    reduce_scatter x1, waiting for transfers between devices, body(): return lax.psum_scatter(combined, 'hid', scatter_dimension=0, tiled=True)  14.9 us
  transfers between devices with their start and end apart: 2, of which 2 were waited for; matrix products, arithmetic and copies ran while one was open for 4% of the time, Pallas kernels for 0%

profile of v1, /device:TPU:0, one launch (start us, length us, event | category | flops | bytes accessed | tf_op | source)
XLA Modules:
  0.0 327.6 jit_solution(2800990674379746930)
XLA Ops:
  6.5 0.0 all-gather.2.cloned.1.call-start
  6.5 0.7 all-gather.2.cloned.1.call-update
  7.3 0.0 reduce-scatter.2.cloned.1.call-start
  7.3 1.1 copy.14
  8.4 0.0 copy-start.1
  8.4 0.5 eq.18
  8.9 4.6 %reduce-window.6 = s32[16,32,128]{2,1,0:T(8,128)S(1)} reduce-window(s32[16,32,128]{2,1,0:T(8,128)S(1)} %fusion, s32[]{:T(128)} %constant.22.clone.1), window={size=1x1x128 pad=0_0x0_0x127_0}, to_apply=%region_0.0 | reduce-window | flops 8323072 | bytes 524292 | tf_op jit(solution)/shard_map/reduce-window
  13.5 0.5 slice_reduce_fusion
  14.0 0.2 reduce-window.9
  14.2 0.1 broadcast_add_fusion
  14.3 0.6 copy.18
  15.0 0.1 select_reduce_fusion.1
  15.1 0.2 select_reduce_fusion
  15.2 1.0 reshape.60.place
  16.2 0.0 copy-start
  16.3 0.9 copy.16
  17.2 0.0 copy-done.1
  17.2 1.3 copy.17.scale
  18.5 0.6 pad_add_fusion.table
  19.1 5.4 %all-gather.2.cloned.1.call-done.tokens = bf16[2048,896]{1,0:T(8,128)(2,1)} async-done(((bf16[1024,896]{1,0:T(8,128)(2,1)}), bf16[2048,896]{1,0:T(8,128)(2,1)}) %all-gather.2.cloned.1.call-update) | async-done | bytes 3670032 | tf_op jit(solution)/shard_map/all_gather | solution.py:236
  24.5 48.6 %shard_map.64.partial = bf16[4,4736,256]{2,1,0:T(8,128)(2,1)} custom-call(s32[32]{0:T(128)} %pad_add_fusion.table, s32[2,2048]{1,0:T(2,128)} %bitcast.11, bf16[2048,896]{1,0:T(8,128)(2,1)} %all-gather.2.cloned.1.call-done.tokens, bf16[16,896,512]{2,1,0:T(8,128)(2,1)} %gate.1, bf16[16,896,512]{2,1,0:T(8,128)(2,1)} %up.1), custom_call_target="tpu_custom_call" | custom-call | tf_op jit(solution)/shard_map/pallas_call | solution.py:238
  73.2 0.0 copy-done
  73.2 191.4 %shard_map.65.hidden = bf16[4,4736,128]{2,1,0:T(8,128)(2,1)} custom-call(bf16[4,4736,256]{2,1,0:T(8,128)(2,1)} %shard_map.64.partial), custom_call_target="tpu_custom_call" | custom-call | tf_op jit(solution)/shard_map/pallas_call | solution.py:257
  264.5 41.3 %shard_map.66 = bf16[2048,896]{1,0:T(8,128)(2,1)} custom-call(s32[32]{0:T(128)} %pad_add_fusion.table, s32[2048,2]{1,0:T(8,128)} %copy-done, f32[2048,2]{1,0:T(8,128)} %copy.17.scale, bf16[4,4736,128]{2,1,0:T(8,128)(2,1)} %shard_map.65.hidden, bf16[16,512,896]{2,1,0:T(8,128)(2,1)} %weight.1), custom_call_target="tpu_custom_call" | custom-call | tf_op jit(solution)/shard_map/pallas_call | solution.py:283
  305.9 0.0 reduce-scatter.2.cloned.1.call-update
  305.9 14.9 %reduce-scatter.2.cloned.1.call-done = bf16[1024,896]{1,0:T(8,128)(2,1)} async-done(((bf16[2048,896]{1,0:T(8,128)(2,1)}), bf16[1024,896]{1,0:T(8,128)(2,1)}) %reduce-scatter.2.cloned.1.call-update) | async-done | bytes 1835024 | tf_op jit(solution)/shard_map/reduce_scatter | solution.py:300
  (3 shorter events, 0.0 us)
Async XLA Ops:
  6.5 18.0 %all-gather.2.cloned.1.call-start = ((), (), s32[]{:S(2)}) async-start(), calls=%async_computation.1 | async-start | bytes 5505024 | tf_op jit(solution)/shard_map/all_gather | solution.py:236
  7.3 313.5 %reduce-scatter.2.cloned.1.call-start = ((), (), s32[]{:S(2)}) async-start(), calls=%async_computation.2 | async-start | bytes 5505024 | tf_op jit(solution)/shard_map/reduce_scatter | solution.py:300
  8.4 8.8 %copy-start.1 = (f32[2048,2]{0,1:T(2,128)S(1)}, f32[2048,2]{0,1:T(2,128)}, u32[]{:S(2)}) copy-start(f32[2048,2]{0,1:T(2,128)} %param.8) | copy-start | bytes 49156
  16.2 56.9 %copy-start = (s32[2048,2]{1,0:T(8,128)}, s32[2048,2]{1,0:T(8,128)S(1)}, u32[]{:S(2)}) copy-start(s32[2048,2]{1,0:T(8,128)S(1)} %reshape.60.place) | copy-start | bytes 49156
Sparse Core Ops, SparseCore 0:
  8.9 15.5 all-gather.1
  306.0 14.7 reduce-scatter.1

commit v2 on v1

v2 whole, which is shorter than its diff:
```python
import functools

import jax
import jax.numpy as jnp
from jax import lax
from jax.experimental import pallas as pl
from jax.experimental.pallas import tpu as pltpu
from jax.sharding import PartitionSpec as P

row_align = 16
lane_width = 128
row_unit = 256
combine_step = 512
y_window = 3
vmem_bytes = 60 * 1024 * 1024


def round_up(value, unit):
    return (value + unit - 1) // unit * unit


def routing_tables(expert_ids, experts):
    flat_ids = expert_ids.reshape(-1)
    labels = jnp.arange(experts, dtype=jnp.int32)
    onehot = (labels[:, None] == flat_ids[None, :]).astype(jnp.int32)
    running = jnp.cumsum(onehot, axis=1)
    counts = running[:, -1]
    padded = (counts + row_align - 1) // row_align * row_align
    starts = jnp.sum(jnp.where(labels[None, :] < labels[:, None], padded[None, :], 0), axis=1)
    place = jnp.sum(onehot * (running - 1 + starts[:, None]), axis=0)
    return place.reshape(expert_ids.shape), jnp.concatenate([starts, counts]).astype(jnp.int32)


def up_kernel(experts, real_rows, rows, step_rows, block, table, place, mine, peer, gate, up, out, gathered):
    expert = pl.program_id(0)
    half = mine.shape[0]

    @pl.when(expert == 0)
    def _():
        tail = gathered.shape[0] - rows
        gathered[rows:, :] = jnp.zeros((tail, gathered.shape[1]), gathered.dtype)
        rest = out.shape[1] - real_rows
        out[:, real_rows:, :] = jnp.zeros((out.shape[0], rest, out.shape[2]), out.dtype)
        first, second = place[0:1, :], place[1:2, :]

        def gather(step, carry):
            base = pl.multiple_of(step * step_rows, row_align)
            ids = lax.broadcasted_iota(jnp.int32, (step_rows, 2 * half), 0) + base
            chosen = jnp.where((ids == first) | (ids == second), 1.0, 0.0).astype(jnp.bfloat16)
            picked = jnp.dot(chosen[:, :half], mine[...], preferred_element_type=jnp.float32)
            picked += jnp.dot(chosen[:, half:], peer[...], preferred_element_type=jnp.float32)
            gathered[pl.ds(base, step_rows), :] = picked.astype(jnp.bfloat16)
            return carry

        lax.fori_loop(0, rows // step_rows, gather, 0)

    base = pl.multiple_of(table[expert], row_align)
    part = gathered[pl.ds(base, block), :]
    gates = jnp.dot(part, gate[0], preferred_element_type=jnp.float32).astype(jnp.bfloat16)
    ups = jnp.dot(part, up[0], preferred_element_type=jnp.float32).astype(jnp.bfloat16)
    for s in range(out.shape[0]):
        cut = slice(s * lane_width, (s + 1) * lane_width)
        out[s, pl.ds(base, block), 0:lane_width] = gates[:, cut]
        out[s, pl.ds(base, block), lane_width:] = ups[:, cut]


def exchange_kernel(n, rows, partial, result, own, paired, summed, hidden, *sems):
    own_sem, y_send, y_recv, z_send, z_recv, g_send, g_recv, h_send, h_recv, out_sem = sems
    slices = own.shape[0]
    depth = n // 2
    chunk = rows // n
    half = rows // 2
    me = lax.axis_index("wide")
    y, z = lax.rem(me, 2), lax.div(me, 2)
    y_peer = {"wide": me + 1 - 2 * y}
    ahead = [{"wide": lax.rem(z + j, depth) * 2 + y} for j in range(depth)]
    mesh_type = pl.DeviceIdType.MESH

    def span(base, j):
        return pl.ds(pl.multiple_of(base + lax.rem(z + j, depth) * chunk, row_align), chunk)

    own_base = y * half
    peer_base = (1 - y) * half

    def own_copy(s):
        return pltpu.make_async_copy(
            partial.at[s, pl.ds(pl.multiple_of(own_base, row_align), half)],
            own.at[s], own_sem.at[s],
        )

    def y_copy(s, j):
        return pltpu.make_async_remote_copy(
            partial.at[s, span(peer_base, j)], paired.at[s, span(0, j)],
            y_send.at[s, j], y_recv.at[s, j], y_peer, mesh_type,
        )

    def z_copy(s, j):
        return pltpu.make_async_remote_copy(
            own.at[s, span(0, j)], summed.at[s, j - 1],
            z_send.at[s, j - 1], z_recv.at[s, j - 1], ahead[j], mesh_type,
        )

    def g_copy(s, j):
        return pltpu.make_async_remote_copy(
            hidden.at[s, span(own_base, 0)], hidden.at[s, span(own_base, 0)],
            g_send.at[s, j - 1], g_recv.at[s, j - 1], ahead[j], mesh_type,
        )

    def h_copy(s, j):
        rows_of = span(own_base, depth - j)
        return pltpu.make_async_remote_copy(
            hidden.at[s, rows_of], hidden.at[s, rows_of],
            h_send.at[s, j], h_recv.at[s, j], y_peer, mesh_type,
        )

    def out_copy(s):
        return pltpu.make_async_copy(
            hidden.at[s], result.at[s, pl.ds(0, rows)], out_sem.at[s]
        )

    barrier = pltpu.get_barrier_semaphore()
    for peer in [y_peer] + ahead[1:]:
        pl.semaphore_signal(barrier, inc=1, device_id=peer, device_id_type=mesh_type)
    for s in range(slices):
        own_copy(s).start()
    pl.semaphore_wait(barrier, depth)
    far_first = sorted(range(1, depth), key=lambda j: -min(j, depth - j))
    near_first = far_first[::-1]
    pieces = [(s, j) for s in range(slices) for j in far_first + [0]]
    for s, j in pieces[:y_window]:
        y_copy(s, j).start()

    def reduce(s):
        total = own[s, span(0, 0)].astype(jnp.float32)
        for j in near_first:
            z_copy(s, j).wait_recv()
        for j in near_first:
            total = total + summed[s, j - 1].astype(jnp.float32)
        gates, ups = total[:, :lane_width], total[:, lane_width:]
        hidden[s, span(own_base, 0)] = (gates / (1.0 + jnp.exp(-gates)) * ups).astype(jnp.bfloat16)
        for j in far_first:
            g_copy(s, j).start()
        h_copy(s, 0).start()

    def forward(s):
        for j in near_first:
            g_copy(s, j).wait_recv()
            h_copy(s, j).start()

    def finish(s):
        for j in range(depth):
            h_copy(s, j).wait_recv()
        out_copy(s).start()

    for step in range(slices + 3):
        if step < slices:
            own_copy(step).wait()
            for k in range(step * depth, (step + 1) * depth):
                s, j = pieces[k]
                y_copy(s, j).wait_recv()
                if k + y_window < len(pieces):
                    y_copy(*pieces[k + y_window]).start()
                part = span(0, j)
                own[s, part] = (
                    own[s, part].astype(jnp.float32) + paired[s, part].astype(jnp.float32)
                ).astype(jnp.bfloat16)
                if j > 0:
                    z_copy(s, j).start()
        if 0 <= step - 2 < slices:
            forward(step - 2)
        if 0 <= step - 1 < slices:
            reduce(step - 1)
        if 0 <= step - 3 < slices:
            finish(step - 3)
    for s in range(slices):
        for j in range(depth):
            y_copy(s, j).wait_send()
            h_copy(s, j).wait_send()
        for j in range(1, depth):
            z_copy(s, j).wait_send()
            g_copy(s, j).wait_send()
        out_copy(s).wait()


def combine_rows(rows, place, scale, held, out):
    def combine(step, carry):
        span = pl.ds(pl.multiple_of(step * combine_step, combine_step), combine_step)
        ids = lax.broadcasted_iota(jnp.int32, (combine_step, rows), 1)
        places, scales = place[span, :], scale[span, :]
        mixed = jnp.where(
            ids == places[:, 0:1], scales[:, 0:1],
            jnp.where(ids == places[:, 1:2], scales[:, 1:2], 0.0),
        ).astype(jnp.bfloat16)
        total = jnp.dot(mixed, held[0:rows, :], preferred_element_type=jnp.float32)
        out[span, :] = total.astype(out.dtype)
        return carry

    lax.fori_loop(0, out.shape[0] // combine_step, combine, 0)


def down_kernel(experts, real_rows, rows, block, table, place, scale, hidden, weight, out, held):
    expert = pl.program_id(0)

    @pl.when(expert == 0)
    def _():
        rest = held.shape[0] - real_rows
        held[real_rows:, :] = jnp.zeros((rest, held.shape[1]), held.dtype)

    base = pl.multiple_of(table[expert], row_align)
    part = jnp.concatenate(
        [hidden[s, pl.ds(base, block), :] for s in range(hidden.shape[0])], axis=1
    )
    product = jnp.dot(part, weight[0], preferred_element_type=jnp.float32)
    held[pl.ds(base, block), :] = product.astype(jnp.bfloat16)

    @pl.when(expert == experts - 1)
    def _():
        combine_rows(rows, place, scale, held, out)


def own_kernel(rows, place, scale, held, out):
    combine_rows(rows, place, scale, held, out)


def whole_block(shape):
    return pl.BlockSpec(
        shape, lambda e, table: (0,) * len(shape), pipeline_mode=pl.Buffered(1)
    )


def body(n, tokens, expert_ids, gate_scale, gate_weight, up_weight, down_weight):
    token_total, slot_count = expert_ids.shape
    experts, width, half_hidden = gate_weight.shape
    slices = half_hidden // lane_width
    depth = n // 2
    real_rows = token_total * slot_count
    capacity = round_up(real_rows * 3 // (2 * experts), 2 * row_align)
    block = capacity
    half_tokens = token_total // 2
    swap = [(0, 1), (1, 0)]
    rows = round_up(real_rows + row_align * experts, max(n * row_align, row_unit))
    chunk = rows // n
    all_rows = rows + capacity
    bf16 = jnp.bfloat16

    place, table = routing_tables(expert_ids, experts)
    peer_tokens = lax.ppermute(tokens, "hid", swap)
    shift = lax.axis_index("hid") * half_tokens
    own_place = lax.dynamic_slice_in_dim(place, shift, half_tokens)
    peer_place = lax.dynamic_slice_in_dim(place, half_tokens - shift, half_tokens)
    own_scale = lax.dynamic_slice_in_dim(gate_scale, shift, half_tokens)
    peer_scale = lax.dynamic_slice_in_dim(gate_scale, half_tokens - shift, half_tokens)
    local_place = jnp.concatenate([own_place, peer_place]).T

    partial = pl.pallas_call(
        functools.partial(up_kernel, experts, real_rows, rows, chunk, block),
        out_shape=jax.ShapeDtypeStruct((slices, all_rows, 2 * lane_width), bf16),
        grid_spec=pltpu.PrefetchScalarGridSpec(
            num_scalar_prefetch=1,
            grid=(experts,),
            in_specs=[
                whole_block((slot_count, token_total)),
                whole_block((half_tokens, width)),
                whole_block((half_tokens, width)),
                pl.BlockSpec((1, width, half_hidden), lambda e, table: (e, 0, 0)),
                pl.BlockSpec((1, width, half_hidden), lambda e, table: (e, 0, 0)),
            ],
            out_specs=whole_block((slices, all_rows, 2 * lane_width)),
            scratch_shapes=[pltpu.VMEM((all_rows, width), bf16)],
        ),
        compiler_params=pltpu.CompilerParams(vmem_limit_bytes=vmem_bytes),
    )(table, local_place, tokens, peer_tokens, gate_weight, up_weight)

    dma = pltpu.SemaphoreType.DMA
    hidden = pl.pallas_call(
        functools.partial(exchange_kernel, n, rows),
        out_shape=jax.ShapeDtypeStruct((slices, all_rows, lane_width), bf16),
        in_specs=[pl.BlockSpec(memory_space=pl.ANY)],
        out_specs=pl.BlockSpec(memory_space=pl.ANY),
        scratch_shapes=[
            pltpu.VMEM((slices, rows // 2, 2 * lane_width), bf16),
            pltpu.VMEM((slices, rows // 2, 2 * lane_width), bf16),
            pltpu.VMEM((slices, depth - 1, chunk, 2 * lane_width), bf16),
            pltpu.VMEM((slices, rows, lane_width), bf16),
            dma((slices,)),
            dma((slices, depth)),
            dma((slices, depth)),
            dma((slices, depth - 1)),
            dma((slices, depth - 1)),
            dma((slices, depth - 1)),
            dma((slices, depth - 1)),
            dma((slices, depth)),
            dma((slices, depth)),
            dma((slices,)),
        ],
        compiler_params=pltpu.CompilerParams(
            collective_id=0, has_side_effects=True, vmem_limit_bytes=vmem_bytes
        ),
    )(partial)

    peer_sum, held = pl.pallas_call(
        functools.partial(down_kernel, experts, real_rows, rows, block),
        out_shape=[
            jax.ShapeDtypeStruct((half_tokens, width), bf16),
            jax.ShapeDtypeStruct((all_rows, width), bf16),
        ],
        grid_spec=pltpu.PrefetchScalarGridSpec(
            num_scalar_prefetch=1,
            grid=(experts,),
            in_specs=[
                whole_block((half_tokens, slot_count)),
                whole_block((half_tokens, slot_count)),
                whole_block((slices, all_rows, lane_width)),
                pl.BlockSpec((1, half_hidden, width), lambda e, table: (e, 0, 0)),
            ],
            out_specs=[whole_block((half_tokens, width)), whole_block((all_rows, width))],
        ),
        compiler_params=pltpu.CompilerParams(vmem_limit_bytes=vmem_bytes),
    )(table, peer_place, peer_scale, hidden, down_weight)
    received = lax.ppermute(peer_sum, "hid", swap)
    own_sum = pl.pallas_call(
        functools.partial(own_kernel, rows),
        out_shape=jax.ShapeDtypeStruct((half_tokens, width), jnp.float32),
        in_specs=[pl.BlockSpec(memory_space=pltpu.VMEM)] * 3,
        out_specs=pl.BlockSpec(memory_space=pltpu.VMEM),
        compiler_params=pltpu.CompilerParams(vmem_limit_bytes=vmem_bytes),
        cost_estimate=pl.CostEstimate(
            flops=2 * half_tokens * rows * width,
            bytes_accessed=2 * all_rows * width,
            transcendentals=0,
        ),
    )(own_place, own_scale, held)
    return (own_sum + received.astype(jnp.float32)).astype(bf16)


def solution(mesh):
    placed = (
        P(("groups", "hid"), "wide"),
        P("groups", None),
        P("groups", None),
        P(None, "wide", "hid"),
        P(None, "wide", "hid"),
        P(None, "hid", "wide"),
    )
    return jax.shard_map(
        functools.partial(body, mesh.shape["wide"]),
        mesh=mesh,
        in_specs=placed,
        out_specs=P(("groups", "hid"), "wide"),
        check_vma=False,
    )
```

time: 329 us -> 286 us (0.87); the launches traced: 328 us -> 281 us
  waiting for transfers between devices: 21 us -> 0.01 us
  Pallas kernels: 281 us -> 262 us
  between operations: 13.5 us -> 0.11 us
  other arithmetic: 5.86 us -> 10.2 us
    pallas_call x1, Pallas kernels: 191 us -> 168 us  [body(): pl.pallas_call(functools.partial(exchange_kernel, n, rows), out_shape=jax...]
    reduce_scatter x1 -> x0, waiting for transfers between devices: 14.9 us -> none  [body(): return lax.psum_scatter(combined, 'hid', scatter_dimension=0, tiled=True)]
    pallas_call x1 -> x2, Pallas kernels: 48.6 us -> 62.1 us  [the longest x1 46.6 us: body(): pl.pallas_call(functools.partial(up_kernel, experts, real_rows, rows, chu...]
    pallas_call x1, Pallas kernels: 41.3 us -> 31.6 us  [body(): pl.pallas_call(functools.partial(down_kernel, experts, real_rows, rows, b...]
    all_gather x1 -> x0, waiting for transfers between devices: 5.39 us -> none  [body(): features = lax.all_gather(tokens, 'hid', axis=0, tiled=True)]
    convert_element_type x0 -> x1, other arithmetic: none -> 3.72 us  [body(): return (own_sum + received.astype(jnp.float32)).astype(bf16)]
  transfers between devices with their start and end apart: 2 -> 2, of which waited for: 2 -> 0; matrix products, arithmetic and copies ran while one was open for 4% -> 5% of each run, Pallas kernels for 0% -> 6%
where the time goes in v2:
time: 286 us; the launch traced here: 281 us
  Pallas kernels  262 us (92%)
  other arithmetic  10.2 us (4%)
  local copies, waits for them, and re-layouts  8.09 us (3%)
    pallas_call x1, Pallas kernels, body(): pl.pallas_call(functools.partial(exchange_kernel, n, rows), out_shape=jax...  168 us
    pallas_call x1, Pallas kernels, body(): pl.pallas_call(functools.partial(up_kernel, experts, real_rows, rows, chu...  46.6 us
    pallas_call x1, Pallas kernels, body(): pl.pallas_call(functools.partial(down_kernel, experts, real_rows, rows, b...  31.6 us
    pallas_call x1, Pallas kernels, body(): pl.pallas_call(functools.partial(own_kernel, rows), out_shape=jax.ShapeDt...  15.5 us
  transfers between devices with their start and end apart: 2, of which 0 were waited for; matrix products, arithmetic and copies ran while one was open for 5% of the time, Pallas kernels for 6%

profile of v2, /device:TPU:0, one launch (start us, length us, event | category | flops | bytes accessed | tf_op | source)
XLA Modules:
  0.0 281.0 jit_solution(13696467053876179238)
XLA Ops:
  0.0 0.5 collective-permute-start
  0.5 1.1 copy.22
  1.5 0.5 eq.18
  2.0 4.6 %reduce-window.6 = s32[16,32,128]{2,1,0:T(8,128)S(1)} reduce-window(s32[16,32,128]{2,1,0:T(8,128)S(1)} %fusion, s32[]{:T(128)} %constant.28.clone.1), window={size=1x1x128 pad=0_0x0_0x127_0}, to_apply=%region_0.0 | reduce-window | flops 8323072 | bytes 524292 | tf_op jit(solution)/shard_map/reduce-window
  6.7 0.5 slice_reduce_fusion
  7.1 0.2 reduce-window.9
  7.3 0.0 copy-start.3
  7.3 0.1 broadcast_add_fusion
  7.5 0.6 copy.28
  8.1 0.0 copy-start.1
  8.1 0.1 select_reduce_fusion.1
  8.2 1.2 copy-done.1
  9.4 0.1 select_reduce_fusion
  9.6 1.0 reshape.60
  10.6 0.1 constant_dynamic-slice_fusion.1
  10.7 0.0 copy-start
  10.7 0.0 copy-start.2
  10.7 0.2 copy.26
  10.9 0.2 copy.27
  11.1 0.0 copy-done.3
  11.1 1.1 copy.30.scale
  12.2 0.7 slice_bitcast_fusion
  12.9 0.6 pad_add_fusion.table
  13.4 0.6 add_bitcast_fusion.place
  14.1 0.0 collective-permute-done.peer
  14.1 46.6 %shard_map.64.partial = bf16[4,4736,256]{2,1,0:T(8,128)(2,1)} custom-call(s32[32]{0:T(128)} %pad_add_fusion.table, s32[2,2048]{1,0:T(2,128)} %add_bitcast_fusion.place, bf16[1024,896]{1,0:T(8,128)(2,1)} %mine.1, bf16[1024,896]{1,0:T(8,128)(2,1)} %collective-permute-done.peer, bf16[16,896,512]{2,1,0:T(8,128)(2,1)} %gate.1, bf16[16,896,512]{2,1,0:T(8,128)(2,1)} %up.1), custom_call_target="tpu_custom_call" | custom-call | tf_op jit(solution)/shard_map/pallas_call | solution.py:255
  60.7 0.0 copy-done
  60.7 0.0 copy-done.2
  60.7 168.5 %shard_map.65.hidden = bf16[4,4736,128]{2,1,0:T(8,128)(2,1)} custom-call(bf16[4,4736,256]{2,1,0:T(8,128)(2,1)} %shard_map.64.partial), custom_call_target="tpu_custom_call" | custom-call | tf_op jit(solution)/shard_map/pallas_call | solution.py:275
  229.2 31.6 %shard_map.66 = (bf16[1024,896]{1,0:T(8,128)(2,1)}, bf16[4736,896]{1,0:T(8,128)(2,1)}) custom-call(s32[32]{0:T(128)} %pad_add_fusion.table, s32[1024,2]{1,0:T(8,128)} %copy-done, f32[1024,2]{1,0:T(8,128)} %copy.30.scale, bf16[4,4736,128]{2,1,0:T(8,128)(2,1)} %shard_map.65.hidden, bf16[16,512,896]{2,1,0:T(8,128)(2,1)} %weight.1), custom_call_target="tpu_custom_call" | custom-call | tf_op jit(solution)/shard_map/pallas_call | solution.py:301
  260.8 0.0 collective-permute-start.1
  260.8 1.0 copy.29.scale
  261.8 15.5 %shard_map.67 = f32[1024,896]{1,0:T(8,128)} custom-call(s32[1024,2]{1,0:T(8,128)} %copy-done.2, f32[1024,2]{1,0:T(8,128)} %copy.29.scale, bf16[4736,896]{1,0:T(8,128)(2,1)} %get-tuple-element.7.held), custom_call_target="tpu_custom_call" | custom-call | flops 7985954816 | bytes 8486912 | tf_op jit(solution)/shard_map/pallas_call | solution.py:321
  277.3 0.0 collective-permute-done.1
  277.3 3.7 %add_convert_fusion = bf16[1024,896]{1,0:T(8,128)(2,1)} fusion(f32[1024,896]{1,0:T(8,128)} %shard_map.67, bf16[1024,896]{1,0:T(8,128)(2,1)S(1)} %collective-permute-done.1), kind=kLoop, calls=%fused_computation | loop fusion | flops 2752512 | bytes 7340032 | tf_op jit(solution)/shard_map/convert_element_type | solution.py:333
  (3 shorter events, 0.0 us)
Async XLA Ops:
  0.0 14.1 %collective-permute-start = (bf16[1024,896]{1,0:T(8,128)(2,1)}, bf16[1024,896]{1,0:T(8,128)(2,1)}, u32[]{:S(2)}, u32[]{:S(2)}) collective-permute-start(bf16[1024,896]{1,0:T(8,128)(2,1)} %mine.1), channel_id=1, source_target_pairs={{0,1},{1,0},{2,3},{3,2},{4,5},{5,4},{6,7},{7,6},{8,9},{9,8},{10,11... | collective-permute-start | bytes 5505032 | tf_op jit(solution)/shard_map/ppermute | solution.py:247
  7.3 3.8 %copy-start.3 = (f32[2048,2]{0,1:T(2,128)S(1)}, f32[2048,2]{0,1:T(2,128)}, u32[]{:S(2)}) copy-start(f32[2048,2]{0,1:T(2,128)} %param.8) | copy-start | bytes 49156
  8.1 1.4 copy-start.1
  10.7 50.0 %copy-start = (s32[1024,2]{1,0:T(8,128)}, s32[1024,2]{1,0:T(8,128)S(1)}, u32[]{:S(2)}) copy-start(s32[1024,2]{1,0:T(8,128)S(1)} %get-tuple-element.9.place) | copy-start | bytes 24580
  10.7 50.0 %copy-start.2 = (s32[1024,2]{1,0:T(8,128)}, s32[1024,2]{1,0:T(8,128)S(1)}, u32[]{:S(2)}) copy-start(s32[1024,2]{1,0:T(8,128)S(1)} %get-tuple-element.10.place) | copy-start | bytes 24580
  260.8 16.5 %collective-permute-start.1 = (bf16[1024,896]{1,0:T(8,128)(2,1)}, bf16[1024,896]{1,0:T(8,128)(2,1)S(1)}, u32[]{:S(2)}, u32[]{:S(2)}) collective-permute-start(bf16[1024,896]{1,0:T(8,128)(2,1)} %get-tuple-element.8), channel_id=1, source_target_pairs={{0,1},{1,0},{2,3},{3,2},{4,5},{5,4},{6,7},{7,6},{8,9},{9,8},{10,11... | collective-permute-start | bytes 5505032 | tf_op jit(solution)/shard_map/ppermute | solution.py:320

commit v3 on v2

--- a/solution.py
+++ b/solution.py
@@ -100,17 +100,49 @@
             z_send.at[s, j - 1], z_recv.at[s, j - 1], ahead[j], mesh_type,
         )
 
-    def g_copy(s, j):
-        return pltpu.make_async_remote_copy(
-            hidden.at[s, span(own_base, 0)], hidden.at[s, span(own_base, 0)],
-            g_send.at[s, j - 1], g_recv.at[s, j - 1], ahead[j], mesh_type,
-        )
-
-    def h_copy(s, j):
-        rows_of = span(own_base, depth - j)
+    def chunk_of(base, index):
+        return pl.ds(pl.multiple_of(base + index * chunk, row_align), chunk)
+
+    def g_copy(s, side, hop):
+        source = z - hop + 1 if side == 0 else z + hop - 1
+        target = me + 2 if side == 0 else me - 2
+        rows_of = chunk_of(own_base, source)
         return pltpu.make_async_remote_copy(
             hidden.at[s, rows_of], hidden.at[s, rows_of],
-            h_send.at[s, j], h_recv.at[s, j], y_peer, mesh_type,
+            g_send.at[s, side * depth + hop], g_recv.at[s, side * depth + hop],
+            {"wide": target}, mesh_type,
+        )
+
+    def sends(side, hop):
+        if side == 0:
+            return jnp.logical_and(z < depth - 1, z - hop + 1 >= 0)
+        return jnp.logical_and(z > 0, z + hop - 1 < depth)
+
+    def g_start(s, side, hop):
+        @pl.when(sends(side, hop))
+        def _():
+            g_copy(s, side, hop).start()
+
+    def receives(side, hop):
+        return z - hop >= 0 if side == 0 else z + hop < depth
+
+    def arrived(side, hop):
+        return chunk_of(own_base, z - hop if side == 0 else z + hop)
+
+    def g_wait(s, side, hop):
+        rows_of = arrived(side, hop)
+        pltpu.make_async_remote_copy(
+            hidden.at[s, rows_of], hidden.at[s, rows_of],
+            g_send.at[s, side * depth + hop], g_recv.at[s, side * depth + hop],
+            y_peer, mesh_type,
+        ).wait_recv()
+
+    def h_copy(s, side, hop):
+        rows_of = arrived(side, hop)
+        return pltpu.make_async_remote_copy(
+            hidden.at[s, rows_of], hidden.at[s, rows_of],
+            h_send.at[s, side * depth + hop], h_recv.at[s, side * depth + hop],
+            y_peer, mesh_type,
         )
 
     def out_copy(s):
@@ -138,18 +170,26 @@
             total = total + summed[s, j - 1].astype(jnp.float32)
         gates, ups = total[:, :lane_width], total[:, lane_width:]
         hidden[s, span(own_base, 0)] = (gates / (1.0 + jnp.exp(-gates)) * ups).astype(jnp.bfloat16)
-        for j in far_first:
-            g_copy(s, j).start()
-        h_copy(s, 0).start()
-
-    def forward(s):
-        for j in near_first:
-            g_copy(s, j).wait_recv()
-            h_copy(s, j).start()
+        for side in (0, 1):
+            g_start(s, side, 1)
+        h_copy(s, 0, 0).start()
+
+    def forward(s, hop):
+        for side in (0, 1):
+            @pl.when(receives(side, hop))
+            def _(side=side):
+                g_wait(s, side, hop)
+                if hop + 1 < depth:
+                    g_start(s, side, hop + 1)
+                h_copy(s, side, hop).start()
 
     def finish(s):
-        for j in range(depth):
-            h_copy(s, j).wait_recv()
+        h_copy(s, 0, 0).wait_recv()
+        for side in (0, 1):
+            for hop in range(1, depth):
+                @pl.when(receives(side, hop))
+                def _(side=side, hop=hop):
+                    h_copy(s, side, hop).wait_recv()
         out_copy(s).start()
 
     for step in range(slices + 3):
@@ -166,8 +206,12 @@
                 ).astype(jnp.bfloat16)
                 if j > 0:
                     z_copy(s, j).start()
-        if 0 <= step - 2 < slices:
-            forward(step - 2)
+                hop = k - step * depth
+                if hop > 0 and step >= 2:
+                    forward(step - 2, hop)
+        elif step - 2 < slices:
+            for hop in range(1, depth):
+                forward(step - 2, hop)
         if 0 <= step - 1 < slices:
             reduce(step - 1)
         if 0 <= step - 3 < slices:
@@ -175,10 +219,17 @@
     for s in range(slices):
         for j in range(depth):
             y_copy(s, j).wait_send()
-            h_copy(s, j).wait_send()
+        h_copy(s, 0, 0).wait_send()
         for j in range(1, depth):
             z_copy(s, j).wait_send()
-            g_copy(s, j).wait_send()
+            for side in (0, 1):
+                @pl.when(sends(side, j))
+                def _(s=s, side=side, j=j):
+                    g_copy(s, side, j).wait_send()
+
+                @pl.when(receives(side, j))
+                def _(s=s, side=side, j=j):
+                    h_copy(s, side, j).wait_send()
         out_copy(s).wait()
 
 
@@ -287,10 +338,10 @@
             dma((slices, depth)),
             dma((slices, depth - 1)),
             dma((slices, depth - 1)),
-            dma((slices, depth - 1)),
-            dma((slices, depth - 1)),
-            dma((slices, depth)),
-            dma((slices, depth)),
+            dma((slices, 2 * depth)),
+            dma((slices, 2 * depth)),
+            dma((slices, 2 * depth)),
+            dma((slices, 2 * depth)),
             dma((slices,)),
         ],
         compiler_params=pltpu.CompilerParams(

time: 286 us -> 272 us (0.951); the launches traced: 281 us -> 271 us
  Pallas kernels: 262 us -> 252 us
    pallas_call x1, Pallas kernels: 168 us -> 158 us  [body(): pl.pallas_call(functools.partial(exchange_kernel, n, rows), out_shape=jax...]
where the time goes in v3:
time: 272 us; the launch traced here: 271 us
  Pallas kernels  252 us (93%)
  other arithmetic  10.2 us (4%)
  local copies, waits for them, and re-layouts  8.09 us (3%)
    pallas_call x1, Pallas kernels, body(): pl.pallas_call(functools.partial(exchange_kernel, n, rows), out_shape=jax...  158 us
    pallas_call x1, Pallas kernels, body(): pl.pallas_call(functools.partial(up_kernel, experts, real_rows, rows, chu...  46.7 us
    pallas_call x1, Pallas kernels, body(): pl.pallas_call(functools.partial(down_kernel, experts, real_rows, rows, b...  31.6 us
    pallas_call x1, Pallas kernels, body(): pl.pallas_call(functools.partial(own_kernel, rows), out_shape=jax.ShapeDt...  15.5 us
  transfers between devices with their start and end apart: 2, of which 0 were waited for; matrix products, arithmetic and copies ran while one was open for 5% of the time, Pallas kernels for 6%

profile of v3, /device:TPU:0, one launch (start us, length us, event | category | flops | bytes accessed | tf_op | source)
XLA Modules:
  0.0 270.6 jit_solution(3632274637651574513)
XLA Ops:
  0.0 0.5 collective-permute-start
  0.5 1.1 copy.22
  1.5 0.5 eq.18
  2.0 4.6 %reduce-window.6 = s32[16,32,128]{2,1,0:T(8,128)S(1)} reduce-window(s32[16,32,128]{2,1,0:T(8,128)S(1)} %fusion, s32[]{:T(128)} %constant.28.clone.1), window={size=1x1x128 pad=0_0x0_0x127_0}, to_apply=%region_0.0 | reduce-window | flops 8323072 | bytes 524292 | tf_op jit(solution)/shard_map/reduce-window
  6.7 0.5 slice_reduce_fusion
  7.1 0.2 reduce-window.9
  7.3 0.0 copy-start.3
  7.3 0.1 broadcast_add_fusion
  7.5 0.6 copy.28
  8.1 0.0 copy-start.1
  8.1 0.1 select_reduce_fusion.1
  8.2 1.2 copy-done.1
  9.4 0.1 select_reduce_fusion
  9.6 1.0 reshape.60
  10.6 0.1 constant_dynamic-slice_fusion.1
  10.7 0.0 copy-start
  10.7 0.0 copy-start.2
  10.7 0.2 copy.26
  10.9 0.2 copy.27
  11.1 0.0 copy-done.3
  11.1 1.1 copy.30.scale
  12.2 0.7 slice_bitcast_fusion
  12.9 0.6 pad_add_fusion.table
  13.4 0.6 add_bitcast_fusion.place
  14.1 0.0 collective-permute-done.peer
  14.1 46.7 %shard_map.64.partial = bf16[4,4736,256]{2,1,0:T(8,128)(2,1)} custom-call(s32[32]{0:T(128)} %pad_add_fusion.table, s32[2,2048]{1,0:T(2,128)} %add_bitcast_fusion.place, bf16[1024,896]{1,0:T(8,128)(2,1)} %mine.1, bf16[1024,896]{1,0:T(8,128)(2,1)} %collective-permute-done.peer, bf16[16,896,512]{2,1,0:T(8,128)(2,1)} %gate.1, bf16[16,896,512]{2,1,0:T(8,128)(2,1)} %up.1), custom_call_target="tpu_custom_call" | custom-call | tf_op jit(solution)/shard_map/pallas_call | solution.py:306
  60.7 0.0 copy-done
  60.7 0.0 copy-done.2
  60.7 158.0 %shard_map.65.hidden = bf16[4,4736,128]{2,1,0:T(8,128)(2,1)} custom-call(bf16[4,4736,256]{2,1,0:T(8,128)(2,1)} %shard_map.64.partial), custom_call_target="tpu_custom_call" | custom-call | tf_op jit(solution)/shard_map/pallas_call | solution.py:326
  218.8 31.6 %shard_map.66 = (bf16[1024,896]{1,0:T(8,128)(2,1)}, bf16[4736,896]{1,0:T(8,128)(2,1)}) custom-call(s32[32]{0:T(128)} %pad_add_fusion.table, s32[1024,2]{1,0:T(8,128)} %copy-done, f32[1024,2]{1,0:T(8,128)} %copy.30.scale, bf16[4,4736,128]{2,1,0:T(8,128)(2,1)} %shard_map.65.hidden, bf16[16,512,896]{2,1,0:T(8,128)(2,1)} %weight.1), custom_call_target="tpu_custom_call" | custom-call | tf_op jit(solution)/shard_map/pallas_call | solution.py:352
  250.3 0.0 collective-permute-start.1
  250.3 1.0 copy.29.scale
  251.4 15.5 %shard_map.67 = f32[1024,896]{1,0:T(8,128)} custom-call(s32[1024,2]{1,0:T(8,128)} %copy-done.2, f32[1024,2]{1,0:T(8,128)} %copy.29.scale, bf16[4736,896]{1,0:T(8,128)(2,1)} %get-tuple-element.7.held), custom_call_target="tpu_custom_call" | custom-call | flops 7985954816 | bytes 8486912 | tf_op jit(solution)/shard_map/pallas_call | solution.py:372
  266.8 0.0 collective-permute-done.1
  266.9 3.7 %add_convert_fusion = bf16[1024,896]{1,0:T(8,128)(2,1)} fusion(f32[1024,896]{1,0:T(8,128)} %shard_map.67, bf16[1024,896]{1,0:T(8,128)(2,1)S(1)} %collective-permute-done.1), kind=kLoop, calls=%fused_computation | loop fusion | flops 2752512 | bytes 7340032 | tf_op jit(solution)/shard_map/convert_element_type | solution.py:384
  (3 shorter events, 0.0 us)
Async XLA Ops:
  0.0 14.1 %collective-permute-start = (bf16[1024,896]{1,0:T(8,128)(2,1)}, bf16[1024,896]{1,0:T(8,128)(2,1)}, u32[]{:S(2)}, u32[]{:S(2)}) collective-permute-start(bf16[1024,896]{1,0:T(8,128)(2,1)} %mine.1), channel_id=1, source_target_pairs={{0,1},{1,0},{2,3},{3,2},{4,5},{5,4},{6,7},{7,6},{8,9},{9,8},{10,11... | collective-permute-start | bytes 5505032 | tf_op jit(solution)/shard_map/ppermute | solution.py:298
  7.3 3.8 %copy-start.3 = (f32[2048,2]{0,1:T(2,128)S(1)}, f32[2048,2]{0,1:T(2,128)}, u32[]{:S(2)}) copy-start(f32[2048,2]{0,1:T(2,128)} %param.8) | copy-start | bytes 49156
  8.1 1.4 copy-start.1
  10.7 50.0 %copy-start = (s32[1024,2]{1,0:T(8,128)}, s32[1024,2]{1,0:T(8,128)S(1)}, u32[]{:S(2)}) copy-start(s32[1024,2]{1,0:T(8,128)S(1)} %get-tuple-element.9.place) | copy-start | bytes 24580
  10.7 50.0 %copy-start.2 = (s32[1024,2]{1,0:T(8,128)}, s32[1024,2]{1,0:T(8,128)S(1)}, u32[]{:S(2)}) copy-start(s32[1024,2]{1,0:T(8,128)S(1)} %get-tuple-element.10.place) | copy-start | bytes 24580
  250.3 16.5 %collective-permute-start.1 = (bf16[1024,896]{1,0:T(8,128)(2,1)}, bf16[1024,896]{1,0:T(8,128)(2,1)S(1)}, u32[]{:S(2)}, u32[]{:S(2)}) collective-permute-start(bf16[1024,896]{1,0:T(8,128)(2,1)} %get-tuple-element.8), channel_id=1, source_target_pairs={{0,1},{1,0},{2,3},{3,2},{4,5},{5,4},{6,7},{7,6},{8,9},{9,8},{10,11... | collective-permute-start | bytes 5505032 | tf_op jit(solution)/shard_map/ppermute | solution.py:371

commit v4 on v3

--- a/solution.py
+++ b/solution.py
@@ -23,7 +23,18 @@
     flat_ids = expert_ids.reshape(-1)
     labels = jnp.arange(experts, dtype=jnp.int32)
     onehot = (labels[:, None] == flat_ids[None, :]).astype(jnp.int32)
-    running = jnp.cumsum(onehot, axis=1)
+    blocks = onehot.reshape(experts, -1, lane_width).astype(jnp.bfloat16)
+    within = jnp.einsum(
+        "ebi,ij->ebj", blocks, jnp.triu(jnp.ones((lane_width, lane_width), jnp.bfloat16)),
+        preferred_element_type=jnp.float32,
+    )
+    block_total = blocks.shape[1]
+    before = jnp.einsum(
+        "eb,bc->ec", within[:, :, -1].astype(jnp.bfloat16),
+        jnp.triu(jnp.ones((block_total, block_total), jnp.bfloat16), 1),
+        preferred_element_type=jnp.float32,
+    )
+    running = (within + before[:, :, None]).reshape(experts, -1).astype(jnp.int32)
     counts = running[:, -1]
     padded = (counts + row_align - 1) // row_align * row_align
     starts = jnp.sum(jnp.where(labels[None, :] < labels[:, None], padded[None, :], 0), axis=1)
@@ -371,7 +382,7 @@
     received = lax.ppermute(peer_sum, "hid", swap)
     own_sum = pl.pallas_call(
         functools.partial(own_kernel, rows),
-        out_shape=jax.ShapeDtypeStruct((half_tokens, width), jnp.float32),
+        out_shape=jax.ShapeDtypeStruct((half_tokens, width), bf16),
         in_specs=[pl.BlockSpec(memory_space=pltpu.VMEM)] * 3,
         out_specs=pl.BlockSpec(memory_space=pltpu.VMEM),
         compiler_params=pltpu.CompilerParams(vmem_limit_bytes=vmem_bytes),
@@ -381,7 +392,7 @@
             transcendentals=0,
         ),
     )(own_place, own_scale, held)
-    return (own_sum + received.astype(jnp.float32)).astype(bf16)
+    return (own_sum.astype(jnp.float32) + received.astype(jnp.float32)).astype(bf16)
 
 
 def solution(mesh):

time: 272 us -> 266 us (0.978)
  other arithmetic: 10.2 us -> 4.84 us
    another operation x3 -> x0, other arithmetic: 4.95 us -> none
  transfers between devices with their start and end apart: 2 -> 2, of which waited for: 0 -> 0; matrix products, arithmetic and copies ran while one was open for 5% -> 3% of each run, Pallas kernels for 6% -> 6%
where the time goes in v4:
time: 266 us; the launch traced here: 265 us
  Pallas kernels  251 us (94%)
  local copies, waits for them, and re-layouts  7.91 us (3%)
  other arithmetic  4.84 us (2%)
    pallas_call x1, Pallas kernels, body(): pl.pallas_call(functools.partial(exchange_kernel, n, rows), out_shape=jax...  158 us
    pallas_call x1, Pallas kernels, body(): pl.pallas_call(functools.partial(up_kernel, experts, real_rows, rows, chu...  46.8 us
    pallas_call x1, Pallas kernels, body(): pl.pallas_call(functools.partial(down_kernel, experts, real_rows, rows, b...  31.6 us
    pallas_call x1, Pallas kernels, body(): pl.pallas_call(functools.partial(own_kernel, rows), out_shape=jax.ShapeDt...  14.9 us
  transfers between devices with their start and end apart: 2, of which 0 were waited for; matrix products, arithmetic and copies ran while one was open for 3% of the time, Pallas kernels for 6%

profile of v4, /device:TPU:0, one launch (start us, length us, event | category | flops | bytes accessed | tf_op | source)
XLA Modules:
  0.0 265.1 jit_solution(3465964117166414852)
XLA Ops:
  0.0 0.5 collective-permute-start
  0.5 1.1 copy.22
  1.5 0.5 eq.18
  2.0 0.2 fusion
  2.3 0.2 fusion.1
  2.5 0.1 fusion.10
  2.6 0.1 add_convert_fusion.1
  2.8 0.6 copy.28
  3.4 0.0 copy-start.1
  3.4 0.1 select_reduce_fusion.1
  3.5 1.2 copy-done.1
  4.8 0.2 select_reduce_fusion
  4.9 0.0 copy-start.3
  4.9 1.0 reshape.54
  5.9 0.1 constant_dynamic-slice_fusion.3
  6.0 0.0 copy-start
  6.0 0.0 copy-start.2
  6.0 0.2 copy.26
  6.2 0.2 copy.27
  6.4 0.0 copy-done.3
  6.4 1.1 copy.30.scale
  7.5 0.7 slice_bitcast_fusion
  8.2 0.6 pad_add_fusion.table
  8.8 0.6 add_bitcast_fusion.place
  9.4 0.0 collective-permute-done.peer
  9.4 46.8 %shard_map.64.partial = bf16[4,4736,256]{2,1,0:T(8,128)(2,1)} custom-call(s32[32]{0:T(128)} %pad_add_fusion.table, s32[2,2048]{1,0:T(2,128)} %add_bitcast_fusion.place, bf16[1024,896]{1,0:T(8,128)(2,1)} %mine.1, bf16[1024,896]{1,0:T(8,128)(2,1)} %collective-permute-done.peer, bf16[16,896,512]{2,1,0:T(8,128)(2,1)} %gate.1, bf16[16,896,512]{2,1,0:T(8,128)(2,1)} %up.1), custom_call_target="tpu_custom_call" | custom-call | tf_op jit(solution)/shard_map/pallas_call | solution.py:317
  56.2 0.0 copy-done
  56.2 0.0 copy-done.2
  56.2 158.0 %shard_map.65.hidden = bf16[4,4736,128]{2,1,0:T(8,128)(2,1)} custom-call(bf16[4,4736,256]{2,1,0:T(8,128)(2,1)} %shard_map.64.partial), custom_call_target="tpu_custom_call" | custom-call | tf_op jit(solution)/shard_map/pallas_call | solution.py:337
  214.3 31.6 %shard_map.66 = (bf16[1024,896]{1,0:T(8,128)(2,1)}, bf16[4736,896]{1,0:T(8,128)(2,1)}) custom-call(s32[32]{0:T(128)} %pad_add_fusion.table, s32[1024,2]{1,0:T(8,128)} %copy-done, f32[1024,2]{1,0:T(8,128)} %copy.30.scale, bf16[4,4736,128]{2,1,0:T(8,128)(2,1)} %shard_map.65.hidden, bf16[16,512,896]{2,1,0:T(8,128)(2,1)} %weight.1), custom_call_target="tpu_custom_call" | custom-call | tf_op jit(solution)/shard_map/pallas_call | solution.py:363
  245.8 0.0 collective-permute-start.1
  245.8 1.1 copy.29.scale
  246.9 14.9 %shard_map.67 = bf16[1024,896]{1,0:T(8,128)(2,1)} custom-call(s32[1024,2]{1,0:T(8,128)} %copy-done.2, f32[1024,2]{1,0:T(8,128)} %copy.29.scale, bf16[4736,896]{1,0:T(8,128)(2,1)} %get-tuple-element.7.held), custom_call_target="tpu_custom_call" | custom-call | flops 7985954816 | bytes 8486912 | tf_op jit(solution)/shard_map/pallas_call | solution.py:383
  261.8 0.0 collective-permute-done.1
  261.8 3.2 %add_convert_fusion = bf16[1024,896]{1,0:T(8,128)(2,1)} fusion(bf16[1024,896]{1,0:T(8,128)(2,1)S(1)} %collective-permute-done.1, bf16[1024,896]{1,0:T(8,128)(2,1)} %shard_map.67), kind=kLoop, calls=%fused_computation | loop fusion | flops 3670016 | bytes 5505024 | tf_op jit(solution)/shard_map/convert_element_type | solution.py:395
  (3 shorter events, 0.0 us)
Async XLA Ops:
  0.0 9.4 %collective-permute-start = (bf16[1024,896]{1,0:T(8,128)(2,1)}, bf16[1024,896]{1,0:T(8,128)(2,1)}, u32[]{:S(2)}, u32[]{:S(2)}) collective-permute-start(bf16[1024,896]{1,0:T(8,128)(2,1)} %mine.1), channel_id=1, source_target_pairs={{0,1},{1,0},{2,3},{3,2},{4,5},{5,4},{6,7},{7,6},{8,9},{9,8},{10,11... | collective-permute-start | bytes 5505032 | tf_op jit(solution)/shard_map/ppermute | solution.py:309
  3.4 1.4 copy-start.1
  4.9 1.5 copy-start.3
  6.0 50.2 %copy-start = (s32[1024,2]{1,0:T(8,128)}, s32[1024,2]{1,0:T(8,128)S(1)}, u32[]{:S(2)}) copy-start(s32[1024,2]{1,0:T(8,128)S(1)} %get-tuple-element.10.place) | copy-start | bytes 24580
  6.0 50.2 %copy-start.2 = (s32[1024,2]{1,0:T(8,128)}, s32[1024,2]{1,0:T(8,128)S(1)}, u32[]{:S(2)}) copy-start(s32[1024,2]{1,0:T(8,128)S(1)} %get-tuple-element.9.place) | copy-start | bytes 24580
  245.8 16.0 %collective-permute-start.1 = (bf16[1024,896]{1,0:T(8,128)(2,1)}, bf16[1024,896]{1,0:T(8,128)(2,1)S(1)}, u32[]{:S(2)}, u32[]{:S(2)}) collective-permute-start(bf16[1024,896]{1,0:T(8,128)(2,1)} %get-tuple-element.8), channel_id=1, source_target_pairs={{0,1},{1,0},{2,3},{3,2},{4,5},{5,4},{6,7},{7,6},{8,9},{9,8},{10,11... | collective-permute-start | bytes 5505032 | tf_op jit(solution)/shard_map/ppermute | solution.py:382
